TPU v7x, 128 devices: a whole 4x4x4 slice. The times are simulated.
128 devices in a mesh: row: 32 (over z, x, core), grp: 4 (over y).
Axes of the slice: x: 4, y: 4, z: 4, core: 2. Of those that a mesh axis runs over, the one named last changes fastest.
Arguments:
- inputs: bfloat16 [1048576, 512], P(('row', 'grp')), may hold values from -6 to 6
- frequencies: bfloat16 [512, 512], replicated, may hold values from -0.25 to 0.25
- phases: float32 [512], replicated, may hold values from -3.140625 to 3.140625
- targets: bfloat16 [1048576, 128], P(('row', 'grp')), may hold values from -9 to 9
Outputs:
- weights: float32 [512, 128], P('grp', 'row')
All inputs are finite; a program needn't handle non-finite values.
Results may differ from a plain program's by a relative error of at most 0.0036.
Values sent between devices are 32-bit elements; how exact they have to be, the bound alone decides.
No kernel may reach another device: no remote copies, remote signals or barrier semaphores. Data moves between devices by JAX's collectives and lax.ppermute only.
A program may use at most 192 MiB of HBM per device.

v0:
```python
import functools

import jax
import jax.numpy as jnp
import numpy as np
from jax import lax
from jax.experimental import pallas as pl
from jax.experimental.pallas import tpu as pltpu
from jax.sharding import Mesh, PartitionSpec as P

CHIPS = ("z", "x", "y")
HIGHEST = lax.Precision.HIGHEST


def dot32(a, b, dims=((1,), (0,))):
    return lax.dot_general(a, b, (dims, ((), ())), precision=HIGHEST, preferred_element_type=jnp.float32)

def halves(v):
    high = v.astype(jnp.bfloat16)
    return high, (v - high.astype(jnp.float32)).astype(jnp.bfloat16)

def dot16(a, b):
    return jnp.dot(a, b, preferred_element_type=jnp.float32)

def dot_split(a, b):
    (ah, al), (bh, bl) = a, b
    return dot16(ah, bh) + (dot16(ah, bl) + dot16(al, bh))

def spectrum_steps(low, high, small):
    middle = 2.0 / (low + high)
    reach = (high - low) / (high + low)
    scales = []
    while reach > small:
        scales.append(2.0 / (2.0 - reach * reach))
        reach = reach * reach / (2.0 - reach * reach)
    return middle, scales

def inverse_of(a, eye, low, high, small=1e-3, polish=2):
    middle, scales = spectrum_steps(low, high, small)
    y = middle * a
    yy = halves(y)
    x = (2.0 * middle * scales[0]) * eye - (middle * scales[0]) * y
    y = scales[0] * (2.0 * y - dot_split(yy, yy))
    for s in scales[1:-1]:
        yy = halves(y); xx = halves(x)
        x = s * (2.0 * x - dot_split(xx, yy))
        y = s * (2.0 * y - dot_split(yy, yy))
    s = scales[-1]
    x = s * (2.0 * x - dot_split(halves(x), halves(y)))
    for _ in range(polish):
        miss = eye - dot32(a, x)
        x = x + dot_split(halves(x), halves(miss))
    return x

def solve_kernel(low, high, ridge, scale, spots_ref, mine_ref, theirs_ref, out_ref, g_ref):
    @pl.when(spots_ref[0] == 0)
    def _():
        g_ref[0] = mine_ref[...]
        g_ref[1] = theirs_ref[...]
    @pl.when(spots_ref[0] != 0)
    def _():
        g_ref[0] = theirs_ref[...]
        g_ref[1] = mine_ref[...]
    rows = lax.broadcasted_iota(jnp.int32, (256, 256), 0)
    cols = lax.broadcasted_iota(jnp.int32, (256, 256), 1)
    eye = jnp.where(rows == cols, 1.0, 0.0).astype(jnp.float32)
    a = jnp.concatenate([g_ref[0, :256], g_ref[0, 256:512]], axis=1) + ridge * eye
    b = jnp.concatenate([g_ref[1, :256], g_ref[1, 256:512]], axis=1)
    c = jnp.concatenate([g_ref[1, 512:768], g_ref[1, 768:]], axis=1) + ridge * eye
    pick = pl.multiple_of(spots_ref[1], 8)
    r1 = jnp.concatenate([g_ref[0, pl.ds(512 + pick, 8)], g_ref[0, pl.ds(640 + pick, 8)]], axis=1)
    r2 = jnp.concatenate([g_ref[0, pl.ds(768 + pick, 8)], g_ref[0, pl.ds(896 + pick, 8)]], axis=1)
    xa = inverse_of(a, eye, low, high)
    t = dot32(b, xa)
    s = c - dot32(t, b, ((1,), (1,)))
    r2 = r2 - dot32(r1, t, ((1,), (1,)))
    xs = inverse_of(s, eye, low, high)
    w2 = dot32(r2, xs)
    w1 = dot32(r1 - dot32(w2, b), xa)
    w = scale * jnp.concatenate([w1, w2], axis=1)
    w = jnp.where(spots_ref[2] == 0, w[:4], w[4:])
    block = spots_ref[3]
    out = w[:, :128]
    for k in range(1, 4):
        out = jnp.where(block == k, w[:, 128 * k:128 * (k + 1)], out)
    out_ref[...] = out

def solve(spots, mine, theirs, ridge, scale):
    low = 0.98 * ridge
    high = 1.01 * (256 * 8 + 1) * ridge
    return pl.pallas_call(
        functools.partial(solve_kernel, low, high, ridge, scale),
        out_shape=jax.ShapeDtypeStruct((4, 128), jnp.float32),
        in_specs=[
            pl.BlockSpec(memory_space=pltpu.SMEM),
            pl.BlockSpec(memory_space=pltpu.VMEM),
            pl.BlockSpec(memory_space=pltpu.VMEM),
        ],
        scratch_shapes=[pltpu.VMEM((2, 1024, 128), jnp.float32)],
        name="solve",
        compiler_params=pltpu.CompilerParams(vmem_limit_bytes=40 * 2**20),
    )(spots, mine, theirs)


def sine_coefficients(scale):
    nodes = np.cos((np.arange(64) + 0.5) * np.pi / 64) * 0.25
    powers = np.stack([nodes ** (2 * k + 1) for k in range(5)], axis=1)
    fitted = np.linalg.lstsq(powers / nodes[:, None], np.sin(2 * np.pi * nodes) / nodes, rcond=None)[0]
    return [float(scale * c) for c in fitted]


def scaled_cosine(angle, scale):
    turns = angle * np.float32(1 / (2 * np.pi))
    turns = turns - jnp.round(turns)
    quarter = 0.25 - jnp.abs(turns)
    square = quarter * quarter
    c = sine_coefficients(scale)
    series = c[3] + square * c[4]
    series = c[2] + square * series
    series = c[1] + square * series
    series = c[0] + square * series
    return quarter * series


def sum_over_devices(parts):
    core = lax.axis_index("core")
    swap = [(0, 1), (1, 0)]
    other = lax.ppermute(lax.dynamic_index_in_dim(parts, 1 - core, keepdims=False), "core", swap)
    half = lax.dynamic_index_in_dim(parts, core, keepdims=False) + other
    chunks = lax.all_to_all(half.reshape(64, 16, 128), CHIPS, 0, 0, tiled=True)
    total = jnp.sum(chunks, axis=0, keepdims=True)
    gathered = lax.all_to_all(jnp.broadcast_to(total, (64, 16, 128)), CHIPS, 0, 0, tiled=True)
    mine = gathered.reshape(1024, 128)
    return mine, lax.ppermute(mine, "core", swap)


def body(inputs, frequencies, phases, targets):
    feature_count = frequencies.shape[1]
    projected = jnp.dot(inputs, frequencies, preferred_element_type=jnp.float32)
    features = scaled_cosine(projected + phases, np.sqrt(2.0 / feature_count)).astype(jnp.bfloat16)

    def cross(a, b):
        return lax.dot_general(a, b, (((0,), (0,)), ((), ())), preferred_element_type=jnp.float32)

    left = features[:, :256]
    late = features[:, 256:]
    a = cross(left, left)
    b = cross(late, features)
    r = cross(targets, features)
    parts = jnp.stack(
        [
            jnp.concatenate([a[:, :128], a[:, 128:], r[:, :128], r[:, 128:256], r[:, 256:384], r[:, 384:]]),
            jnp.concatenate([b[:, :128], b[:, 128:256], b[:, 256:384], b[:, 384:]]),
        ]
    )
    mine, theirs = sum_over_devices(parts)
    total_rows = inputs.shape[0] * 128
    ridge = 0.25 * total_rows / feature_count
    group = lax.axis_index(("z", "x", "core"))
    spots = jnp.stack([lax.axis_index("core"), group // 2 * 8, group % 2, lax.axis_index("y")])
    return solve(spots.astype(jnp.int32), mine, theirs, ridge, np.sqrt(total_rows / feature_count)).T


def solution(mesh):
    split = Mesh(mesh.devices.reshape(4, 4, 2, 4), ("z", "x", "core", "y"))
    rows = ("z", "x", "core", "y")
    return jax.shard_map(
        body,
        mesh=split,
        in_specs=(P(rows, None), P(), P(), P(rows, None)),
        out_specs=P("y", ("z", "x", "core")),
        check_vma=False,
    )
```

profile of v0, /device:TPU:1, one launch (start us, length us, event | category | flops | bytes accessed | tf_op | source)
XLA Modules:
  0.0 87.7 jit_solution(12437971896139072467)
XLA Ops:
  0.0 0.0 copy-start
  0.0 14.4 %multiply_convert_fusion = bf16[8192,512]{1,0:T(8,128)(2,1)S(1)} fusion(bf16[8192,512]{1,0:T(8,128)(2,1)} %param.4, bf16[512,512]{1,0:T(8,128)(2,1)} %param.5, f32[512]{0:T(512)} %param.6), kind=kOutput, calls=%fused_computation.3 | convolution fusion | flops 4366270464 | bytes 17303552 | tf_op jit(solution)/shard_map/dot_general | solution.py:139
  14.4 0.0 copy-start.1
  14.4 1.3 %fusion.6 = f32[256,256]{1,0:T(8,128)S(1)} fusion(bf16[8192,512]{1,0:T(8,128)(2,1)S(1)} %multiply_convert_fusion), kind=kOutput, calls=%fused_computation.10 | convolution fusion | flops 1073741824 | bytes 4456448 | tf_op jit(solution)/shard_map/dot_general | solution.py:143
  15.7 1.9 %copy-done.1 = bf16[8192,512]{1,0:T(8,128)(2,1)} copy-done((bf16[8192,512]{1,0:T(8,128)(2,1)}, bf16[8192,512]{1,0:T(8,128)(2,1)S(1)}, u32[]{:S(2)}) %copy-start.1) | copy-done | bytes 8388632
  17.6 2.3 %fusion.4 = f32[256,512]{1,0:T(8,128)S(1)} fusion(bf16[8192,512]{1,0:T(8,128)(2,1)S(1)} %multiply_convert_fusion), kind=kOutput, calls=%fused_computation.8 | convolution fusion | flops 2147483648 | bytes 13107200 | tf_op jit(solution)/shard_map/dot_general | solution.py:143
  19.9 0.0 copy-done
  19.9 4.8 %convolution_bitcast_fusion = f32[128,512]{1,0:T(8,128)S(1)} fusion(bf16[8192,512]{1,0:T(8,128)(2,1)} %copy-done.1, bf16[8192,128]{1,0:T(8,128)(2,1)S(1)} %copy-done), kind=kOutput, calls=%fused_computation.16 | convolution fusion | flops 1073741824 | bytes 10747904 | tf_op jit(solution)/shard_map/dot_general | solution.py:143
  24.7 0.7 fusion.13
  25.5 0.9 %maximum_bitcast_fusion = f32[1,1024,128]{2,1,0:T(8,128)S(1)} fusion(f32[256,128]{1,0:T(8,128)S(1)} %get-tuple-element.6, f32[256,128]{1,0:T(8,128)S(1)} %get-tuple-element.7, f32[256,128]{1,0:T(8,128)} %get-tuple-element.8, f32[256,128]{1,0:T(8,128)S(1)} %get-tuple-element.5), kind=kLoop, calls=%fused_computation.22 | loop fusion | flops 393216 | bytes 1048576 | tf_op jit(solution)/shard_map/stack | solution.py:150
  26.5 0.9 fusion.9
  27.4 1.4 %collective-permute-start = (f32[1024,128]{1,0:T(8,128)}, f32[1024,128]{1,0:T(8,128)}, u32[]{:S(2)}, u32[]{:S(2)}) collective-permute-start(f32[1024,128]{1,0:T(8,128)} %fusion.9), channel_id=1, source_target_pairs={{0,4},{4,0},{1,5},{5,1},{2,6},{6,2},{3,7},{7,3},{8,12},{12,8},{9,1... | collective-permute-start | bytes 1572872 | tf_op jit(solution)/shard_map/ppermute | solution.py:128
  28.8 1.9 %collective-permute-done = f32[1024,128]{1,0:T(8,128)} collective-permute-done((f32[1024,128]{1,0:T(8,128)}, f32[1024,128]{1,0:T(8,128)}, u32[]{:S(2)}, u32[]{:S(2)}) %collective-permute-start) | collective-permute-done | bytes 524320 | tf_op jit(solution)/shard_map/ppermute | solution.py:128
  30.7 1.1 %fusion.12 = f32[1024,128]{1,0:T(8,128)S(1)} fusion(f32[1024,128]{1,0:T(8,128)} %collective-permute-done, s32[]{:T(128)S(6)} %select_n.20, f32[1,1024,128]{2,1,0:T(8,128)S(1)} %bitcast.26, f32[1,1024,128]{2,1,0:T(8,128)S(1)} %maximum_bitcast_fusion), kind=kLoop, calls=%fused_computation.21 | loop fusion | flops 262144 | bytes 2097156 | tf_op jit(solution)/shard_map/add | solution.py:129
  31.8 23.3 %all_to_all.10 = f32[64,16,128]{2,1,0:T(8,128)S(1)} all-to-all(f32[64,16,128]{2,1,0:T(8,128)S(1)} %bitcast.27), channel_id=1, replica_groups=mesh['z'=4,'x'=4,'core'=2,'y'=4] {'z','x','y'}, dimensions={0} | all-to-all | bytes 1048576 | tf_op jit(solution)/shard_map/all_to_all | solution.py:130
  55.0 0.1 reduce_sum.9
  55.2 15.6 %all_to_all.11 = f32[64,16,128]{2,1,0:T(8,128)S(1)} all-to-all(f32[64,16,128]{2,1,0:T(8,128)S(1)} %broadcast_in_dim.2), channel_id=1, replica_groups=mesh['z'=4,'x'=4,'core'=2,'y'=4] {'z','x','y'}, dimensions={0} | all-to-all | bytes 1048576 | tf_op jit(solution)/shard_map/all_to_all | solution.py:132
  70.8 3.3 %collective-permute-start.1 = (f32[1024,128]{1,0:T(8,128)S(1)}, f32[1024,128]{1,0:T(8,128)S(1)}, u32[]{:S(2)}, u32[]{:S(2)}) collective-permute-start(f32[1024,128]{1,0:T(8,128)S(1)} %bitcast.23), channel_id=1, source_target_pairs={{0,4},{4,0},{1,5},{5,1},{2,6},{6,2},{3,7},{7,3},{8,12},{12,8},{9,1... | collective-permute-start | bytes 1572872 | tf_op jit(solution)/shard_map/ppermute | solution.py:134
  74.1 0.1 pad_add_fusion.spots_ref
  74.1 1.5 %collective-permute-done.1.theirs_ref = f32[1024,128]{1,0:T(8,128)S(1)} collective-permute-done((f32[1024,128]{1,0:T(8,128)S(1)}, f32[1024,128]{1,0:T(8,128)S(1)}, u32[]{:S(2)}, u32[]{:S(2)}) %collective-permute-start.1) | collective-permute-done | bytes 524320 | tf_op jit(solution)/shard_map/ppermute | solution.py:134
  75.6 12.1 %solve.1 = f32[4,128]{1,0:T(4,128)} custom-call(s32[4]{0:T(128)S(1)} %pad_add_fusion.spots_ref, f32[1024,128]{1,0:T(8,128)S(1)} %bitcast.24, f32[1024,128]{1,0:T(8,128)S(1)} %collective-permute-done.1.theirs_ref), custom_call_target="tpu_custom_call" | custom-call | tf_op jit(solution)/shard_map/solve/pallas_call | solution.py:91
  (7 shorter events, 0.1 us)
Async XLA Ops:
  0.0 19.9 %copy-start = (bf16[8192,128]{1,0:T(8,128)(2,1)S(1)}, bf16[8192,128]{1,0:T(8,128)(2,1)}, u32[]{:S(2)}) copy-start(bf16[8192,128]{1,0:T(8,128)(2,1)} %param.7) | copy-start | bytes 6291460
  14.4 3.2 %copy-start.1 = (bf16[8192,512]{1,0:T(8,128)(2,1)}, bf16[8192,512]{1,0:T(8,128)(2,1)S(1)}, u32[]{:S(2)}) copy-start(bf16[8192,512]{1,0:T(8,128)(2,1)S(1)} %multiply_convert_fusion) | copy-start | bytes 25165828
  27.4 3.3 %collective-permute-start = (f32[1024,128]{1,0:T(8,128)}, f32[1024,128]{1,0:T(8,128)}, u32[]{:S(2)}, u32[]{:S(2)}) collective-permute-start(f32[1024,128]{1,0:T(8,128)} %fusion.9), channel_id=1, source_target_pairs={{0,4},{4,0},{1,5},{5,1},{2,6},{6,2},{3,7},{7,3},{8,12},{12,8},{9,1... | collective-permute-start | bytes 1572872 | tf_op jit(solution)/shard_map/ppermute | solution.py:128
  70.8 4.8 %collective-permute-start.1 = (f32[1024,128]{1,0:T(8,128)S(1)}, f32[1024,128]{1,0:T(8,128)S(1)}, u32[]{:S(2)}, u32[]{:S(2)}) collective-permute-start(f32[1024,128]{1,0:T(8,128)S(1)} %bitcast.23), channel_id=1, source_target_pairs={{0,4},{4,0},{1,5},{5,1},{2,6},{6,2},{3,7},{7,3},{8,12},{12,8},{9,1... | collective-permute-start | bytes 1572872 | tf_op jit(solution)/shard_map/ppermute | solution.py:134
where the time goes:
time: 88 us; the launch traced here: 87.7 us
  blocking collectives  38.9 us (44%)
  matrix products  22.8 us (26%)
  Pallas kernels  12.1 us (14%)
  starting transfers between devices  4.72 us (5%)
  waiting for transfers between devices  3.34 us (4%)
  other arithmetic  3.09 us (4%)
  local copies, waits for them, and re-layouts  2.72 us (3%)
    all_to_all x1, blocking collectives, sum_over_devices(): chunks = lax.all_to_all(half.reshape(64, 16, 128), CHIPS, 0, 0, tiled=True)  23.3 us
    all_to_all x1, blocking collectives, sum_over_devices(): lax.all_to_all(jnp.broadcast_to(total, (64, 16, 128)), CHIPS, 0, 0, tiled...  15.6 us
    dot_general x1, matrix products, body(): projected = jnp.dot(inputs, frequencies, preferred_element_type=jnp.float32)  14.4 us
    pallas_call x1, Pallas kernels, solve(): pl.pallas_call(functools.partial(solve_kernel, low, high, ridge, scale),...  12.1 us
    dot_general x3, matrix products, cross(): lax.dot_general(a, b, (((0,), (0,)), ((), ())), preferred_element_type=jn...  8.4 us
    ppermute x1, starting transfers between devices, sum_over_devices(): return (mine, lax.ppermute(mine, 'core', swap))  3.3 us
    unnamed x9, local copies, waits for them, and re-layouts  1.99 us
    ppermute x1, waiting for transfers between devices, sum_over_devices(): lax.ppermute(lax.dynamic_index_in_dim(parts, 1 - core, keepdims=False), '...  1.88 us
  transfers between devices with their start and end apart: 2, of which 2 were waited for; matrix products, arithmetic and copies ran while one was open for 0% of the time, Pallas kernels for 0%

commit v1 on v0

--- a/solution.py
+++ b/solution.py
@@ -104,29 +104,127 @@
 
 def sine_coefficients(scale):
     nodes = np.cos((np.arange(64) + 0.5) * np.pi / 64) * 0.25
-    powers = np.stack([nodes ** (2 * k + 1) for k in range(5)], axis=1)
-    fitted = np.linalg.lstsq(powers / nodes[:, None], np.sin(2 * np.pi * nodes) / nodes, rcond=None)[0]
+    powers = np.stack([nodes ** (2 * k) for k in range(4)], axis=1)
+    fitted = np.linalg.lstsq(powers, np.sin(2 * np.pi * nodes) / nodes, rcond=None)[0]
     return [float(scale * c) for c in fitted]
 
 
-def scaled_cosine(angle, scale):
-    turns = angle * np.float32(1 / (2 * np.pi))
+def cosine_of_turns(turns, scale):
     turns = turns - jnp.round(turns)
     quarter = 0.25 - jnp.abs(turns)
     square = quarter * quarter
     c = sine_coefficients(scale)
-    series = c[3] + square * c[4]
-    series = c[2] + square * series
+    series = c[2] + square * c[3]
     series = c[1] + square * series
     series = c[0] + square * series
     return quarter * series
 
 
-def sum_over_devices(parts):
-    core = lax.axis_index("core")
+def cross(a, b):
+    return lax.dot_general(a, b, (((0,), (0,)), ((), ())), preferred_element_type=jnp.float32)
+
+
+def gram_kernel(blocks, part, scale, spots_ref, x_ref, y_ref, w_ref, phase_ref, send_ref, keep_ref, f_ref, a_ref, b_ref, r_ref):
+    step = pl.program_id(0)
+    rows = x_ref.shape[0]
+    new = lax.rem(step, 2)
+    old = 1 - new
+    turn = np.float32(1 / (2 * np.pi))
+    phase = phase_ref[...] * turn
+
+    def project(s):
+        return jnp.dot(x_ref[s * part:(s + 1) * part], w_ref[...], preferred_element_type=jnp.float32)
+
+    def feature(s, projected):
+        f_ref[new, s * part:(s + 1) * part] = cosine_of_turns(projected * turn + phase, scale).astype(jnp.bfloat16)
+
+    def gram_left():
+        a_ref[...] += cross(f_ref[old, :, :256], f_ref[old, :, :256])
+
+    def gram_rest(k):
+        cols = slice(k * 256, (k + 1) * 256)
+        b_ref[:, cols] += cross(f_ref[old, :, 256:], f_ref[old, :, cols])
+        r_ref[:, cols] += cross(y_ref[...], f_ref[old, :, cols])
+
+    def run(with_features, with_gram):
+        jobs = [gram_left, lambda: gram_rest(0), lambda: gram_rest(1)] if with_gram else []
+        for s in range(rows // part if with_features else 0):
+            projected = project(s)
+            if jobs:
+                jobs.pop(0)()
+            feature(s, projected)
+        for job in jobs:
+            job()
+
+    @pl.when(step == 0)
+    def _():
+        a_ref[...] = jnp.zeros_like(a_ref)
+        b_ref[...] = jnp.zeros_like(b_ref)
+        r_ref[...] = jnp.zeros_like(r_ref)
+        run(True, False)
+
+    @pl.when((step > 0) & (step < blocks))
+    def _():
+        run(True, True)
+
+    @pl.when(step == blocks)
+    def _():
+        run(False, True)
+
+        def first(ref):
+            for k in range(2):
+                ref[256 * k:256 * (k + 1)] = a_ref[:, 128 * k:128 * (k + 1)]
+            for k in range(4):
+                ref[512 + 128 * k:640 + 128 * k] = r_ref[:, 128 * k:128 * (k + 1)]
+
+        def second(ref):
+            for k in range(4):
+                ref[256 * k:256 * (k + 1)] = b_ref[:, 128 * k:128 * (k + 1)]
+
+        @pl.when(spots_ref[0] == 0)
+        def _():
+            first(keep_ref)
+            second(send_ref)
+
+        @pl.when(spots_ref[0] != 0)
+        def _():
+            second(keep_ref)
+            first(send_ref)
+
+
+def in_hbm(array):
+    return pltpu.with_memory_space_constraint(array, pltpu.HBM)
+
+
+def local_gram(spots, inputs, frequencies, phases, targets, rows=1024, part=256):
+    blocks = inputs.shape[0] // rows
+    count = frequencies.shape[1]
+    return pl.pallas_call(
+        functools.partial(gram_kernel, blocks, part, np.sqrt(2.0 / count)),
+        grid=(blocks + 1,),
+        in_specs=[
+            pl.BlockSpec(memory_space=pltpu.SMEM),
+            pl.BlockSpec((rows, 512), lambda i: (jnp.minimum(i, blocks - 1), 0)),
+            pl.BlockSpec((rows, 128), lambda i: (jnp.maximum(i - 1, 0), 0)),
+            pl.BlockSpec((512, 512), lambda i: (0, 0)),
+            pl.BlockSpec((1, 512), lambda i: (0, 0)),
+        ],
+        out_specs=[pl.BlockSpec((1024, 128), lambda i: (0, 0))] * 2,
+        out_shape=[jax.ShapeDtypeStruct((1024, 128), jnp.float32)] * 2,
+        scratch_shapes=[
+            pltpu.VMEM((2, rows, 512), jnp.bfloat16),
+            pltpu.VMEM((256, 256), jnp.float32),
+            pltpu.VMEM((256, 512), jnp.float32),
+            pltpu.VMEM((128, 512), jnp.float32),
+        ],
+        name="gram",
+        compiler_params=pltpu.CompilerParams(vmem_limit_bytes=50 * 2**20),
+    )(spots, inputs, *[in_hbm(v) for v in (targets, frequencies, phases.reshape(1, 512))])
+
+
+def sum_over_devices(send, keep):
     swap = [(0, 1), (1, 0)]
-    other = lax.ppermute(lax.dynamic_index_in_dim(parts, 1 - core, keepdims=False), "core", swap)
-    half = lax.dynamic_index_in_dim(parts, core, keepdims=False) + other
+    half = keep + lax.ppermute(send, "core", swap)
     chunks = lax.all_to_all(half.reshape(64, 16, 128), CHIPS, 0, 0, tiled=True)
     total = jnp.sum(chunks, axis=0, keepdims=True)
     gathered = lax.all_to_all(jnp.broadcast_to(total, (64, 16, 128)), CHIPS, 0, 0, tiled=True)
@@ -136,29 +234,14 @@
 
 def body(inputs, frequencies, phases, targets):
     feature_count = frequencies.shape[1]
-    projected = jnp.dot(inputs, frequencies, preferred_element_type=jnp.float32)
-    features = scaled_cosine(projected + phases, np.sqrt(2.0 / feature_count)).astype(jnp.bfloat16)
-
-    def cross(a, b):
-        return lax.dot_general(a, b, (((0,), (0,)), ((), ())), preferred_element_type=jnp.float32)
-
-    left = features[:, :256]
-    late = features[:, 256:]
-    a = cross(left, left)
-    b = cross(late, features)
-    r = cross(targets, features)
-    parts = jnp.stack(
-        [
-            jnp.concatenate([a[:, :128], a[:, 128:], r[:, :128], r[:, 128:256], r[:, 256:384], r[:, 384:]]),
-            jnp.concatenate([b[:, :128], b[:, 128:256], b[:, 256:384], b[:, 384:]]),
-        ]
-    )
-    mine, theirs = sum_over_devices(parts)
     total_rows = inputs.shape[0] * 128
     ridge = 0.25 * total_rows / feature_count
     group = lax.axis_index(("z", "x", "core"))
     spots = jnp.stack([lax.axis_index("core"), group // 2 * 8, group % 2, lax.axis_index("y")])
-    return solve(spots.astype(jnp.int32), mine, theirs, ridge, np.sqrt(total_rows / feature_count)).T
+    spots = spots.astype(jnp.int32)
+    send, keep = local_gram(spots, inputs, frequencies, phases, targets)
+    mine, theirs = sum_over_devices(send, keep)
+    return solve(spots, mine, theirs, ridge, np.sqrt(total_rows / feature_count)).T
 
 
 def solution(mesh):

time: 88 us -> 76.1 us (0.86)
  matrix products: 22.8 us -> 0 us
  Pallas kernels: 12.1 us -> 29.1 us
  other arithmetic: 3.09 us -> 0.2 us
  local copies, waits for them, and re-layouts: 2.72 us -> 0.04 us
    dot_general x4 -> x0, matrix products: 22.8 us -> none  [the longest x1 14.4 us: body(): projected = jnp.dot(inputs, frequencies, preferred_element_type=jnp.float32)]
    pallas_call x0 -> x1, Pallas kernels: none -> 16.8 us  [local_gram(): pl.pallas_call(functools.partial(gram_kernel, blocks, part, np.sqrt(2.0 /...]
    unnamed x9 -> x0, local copies, waits for them, and re-layouts: 1.99 us -> none
    add x1, other arithmetic: 1.13 us -> 0.05 us  [sum_over_devices(): half = keep + lax.ppermute(send, 'core', swap)]
    another operation x1 -> x0, other arithmetic: 0.94 us -> none  [body(): jnp.stack([jnp.concatenate([a[:, :128], a[:, 128:], r[:, :128], r[:, 128:...]
where the time goes in v1:
time: 76.1 us; the launch traced here: 75.9 us
  blocking collectives  38.7 us (51%)
  Pallas kernels  29.1 us (38%)
  starting transfers between devices  4.79 us (6%)
  waiting for transfers between devices  3.07 us (4%)
    all_to_all x1, blocking collectives, sum_over_devices(): chunks = lax.all_to_all(half.reshape(64, 16, 128), CHIPS, 0, 0, tiled=True)  23.3 us
    pallas_call x1, Pallas kernels, local_gram(): pl.pallas_call(functools.partial(gram_kernel, blocks, part, np.sqrt(2.0 /...  16.8 us
    all_to_all x1, blocking collectives, sum_over_devices(): lax.all_to_all(jnp.broadcast_to(total, (64, 16, 128)), CHIPS, 0, 0, tiled...  15.4 us
    pallas_call x1, Pallas kernels, solve(): pl.pallas_call(functools.partial(solve_kernel, low, high, ridge, scale),...  12.3 us
    ppermute x1, starting transfers between devices, sum_over_devices(): return (mine, lax.ppermute(mine, 'core', swap))  3.3 us
    ppermute x1, waiting for transfers between devices, sum_over_devices(): half = keep + lax.ppermute(send, 'core', swap)  1.54 us
    ppermute x1, waiting for transfers between devices, sum_over_devices(): return (mine, lax.ppermute(mine, 'core', swap))  1.54 us
  transfers between devices with their start and end apart: 2, of which 2 were waited for; matrix products, arithmetic and copies ran while one was open for 0% of the time, Pallas kernels for 0%

profile of v1, /device:TPU:1, one launch (start us, length us, event | category | flops | bytes accessed | tf_op | source)
XLA Modules:
  0.0 75.9 jit_solution(12954754906765790724)
XLA Ops:
  0.0 0.1 pad_add_fusion.spots_ref
  0.1 16.8 %gram.1 = (f32[1024,128]{1,0:T(8,128)S(1)}, f32[1024,128]{1,0:T(8,128)S(1)}) custom-call(s32[4]{0:T(128)S(1)} %pad_add_fusion.spots_ref, bf16[8192,512]{1,0:T(8,128)(2,1)} %x_ref.1, bf16[8192,128]{1,0:T(8,128)(2,1)} %y_ref.1, bf16[512,512]{1,0:T(8,128)(2,1)} %w_ref.1, f32[1,512]{1,0:T(1,128)} %bitcast.11), custom_call_target="tpu_custom_call" | custom-call | tf_op jit(solution)/shard_map/gram/pallas_call | solution.py:202
  16.9 1.5 %collective-permute-start = (f32[1024,128]{1,0:T(8,128)S(1)}, f32[1024,128]{1,0:T(8,128)S(1)}, u32[]{:S(2)}, u32[]{:S(2)}) collective-permute-start(f32[1024,128]{1,0:T(8,128)S(1)} %get-tuple-element.8), channel_id=1, source_target_pairs={{0,4},{4,0},{1,5},{5,1},{2,6},{6,2},{3,7},{7,3},{8,12},{12,8},{9,1... | collective-permute-start | bytes 1572872 | tf_op jit(solution)/shard_map/ppermute | solution.py:227
  18.3 1.5 %collective-permute-done = f32[1024,128]{1,0:T(8,128)S(1)} collective-permute-done((f32[1024,128]{1,0:T(8,128)S(1)}, f32[1024,128]{1,0:T(8,128)S(1)}, u32[]{:S(2)}, u32[]{:S(2)}) %collective-permute-start) | collective-permute-done | bytes 524320 | tf_op jit(solution)/shard_map/ppermute | solution.py:227
  19.9 0.1 add.17
  19.9 23.3 %all_to_all.10 = f32[64,16,128]{2,1,0:T(8,128)S(1)} all-to-all(f32[64,16,128]{2,1,0:T(8,128)S(1)} %bitcast.10), channel_id=1, replica_groups=mesh['z'=4,'x'=4,'core'=2,'y'=4] {'z','x','y'}, dimensions={0} | all-to-all | bytes 1048576 | tf_op jit(solution)/shard_map/all_to_all | solution.py:228
  43.2 0.1 reduce_sum.9
  43.3 15.4 %all_to_all.11 = f32[64,16,128]{2,1,0:T(8,128)S(1)} all-to-all(f32[64,16,128]{2,1,0:T(8,128)S(1)} %broadcast_in_dim.2), channel_id=1, replica_groups=mesh['z'=4,'x'=4,'core'=2,'y'=4] {'z','x','y'}, dimensions={0} | all-to-all | bytes 1048576 | tf_op jit(solution)/shard_map/all_to_all | solution.py:230
  58.7 3.3 %collective-permute-start.1 = (f32[1024,128]{1,0:T(8,128)S(1)}, f32[1024,128]{1,0:T(8,128)S(1)}, u32[]{:S(2)}, u32[]{:S(2)}) collective-permute-start(f32[1024,128]{1,0:T(8,128)S(1)} %bitcast.8), channel_id=1, source_target_pairs={{0,4},{4,0},{1,5},{5,1},{2,6},{6,2},{3,7},{7,3},{8,12},{12,8},{9,1... | collective-permute-start | bytes 1572872 | tf_op jit(solution)/shard_map/ppermute | solution.py:232
  62.0 1.5 %collective-permute-done.1.theirs_ref = f32[1024,128]{1,0:T(8,128)S(1)} collective-permute-done((f32[1024,128]{1,0:T(8,128)S(1)}, f32[1024,128]{1,0:T(8,128)S(1)}, u32[]{:S(2)}, u32[]{:S(2)}) %collective-permute-start.1) | collective-permute-done | bytes 524320 | tf_op jit(solution)/shard_map/ppermute | solution.py:232
  63.6 12.3 %solve.1 = f32[4,128]{1,0:T(4,128)} custom-call(s32[4]{0:T(128)S(1)} %pad_add_fusion.spots_ref, f32[1024,128]{1,0:T(8,128)S(1)} %bitcast.9, f32[1024,128]{1,0:T(8,128)S(1)} %collective-permute-done.1.theirs_ref), custom_call_target="tpu_custom_call" | custom-call | tf_op jit(solution)/shard_map/solve/pallas_call | solution.py:91
  (1 shorter events, 0.0 us)
Async XLA Ops:
  16.9 3.0 %collective-permute-start = (f32[1024,128]{1,0:T(8,128)S(1)}, f32[1024,128]{1,0:T(8,128)S(1)}, u32[]{:S(2)}, u32[]{:S(2)}) collective-permute-start(f32[1024,128]{1,0:T(8,128)S(1)} %get-tuple-element.8), channel_id=1, source_target_pairs={{0,4},{4,0},{1,5},{5,1},{2,6},{6,2},{3,7},{7,3},{8,12},{12,8},{9,1... | collective-permute-start | bytes 1572872 | tf_op jit(solution)/shard_map/ppermute | solution.py:227
  58.7 4.8 %collective-permute-start.1 = (f32[1024,128]{1,0:T(8,128)S(1)}, f32[1024,128]{1,0:T(8,128)S(1)}, u32[]{:S(2)}, u32[]{:S(2)}) collective-permute-start(f32[1024,128]{1,0:T(8,128)S(1)} %bitcast.8), channel_id=1, source_target_pairs={{0,4},{4,0},{1,5},{5,1},{2,6},{6,2},{3,7},{7,3},{8,12},{12,8},{9,1... | collective-permute-start | bytes 1572872 | tf_op jit(solution)/shard_map/ppermute | solution.py:232

commit v2 on v1

--- a/solution.py
+++ b/solution.py
@@ -35,71 +35,98 @@
         reach = reach * reach / (2.0 - reach * reach)
     return middle, scales
 
-def inverse_of(a, eye, low, high, small=1e-3, polish=2):
-    middle, scales = spectrum_steps(low, high, small)
+def inverse_of(a, eye, low, high, polish):
+    middle, scales = spectrum_steps(low, high, 1e-3)
     y = middle * a
     yy = halves(y)
     x = (2.0 * middle * scales[0]) * eye - (middle * scales[0]) * y
     y = scales[0] * (2.0 * y - dot_split(yy, yy))
     for s in scales[1:-1]:
-        yy = halves(y); xx = halves(x)
-        x = s * (2.0 * x - dot_split(xx, yy))
+        yy = halves(y)
+        x = s * (2.0 * x - dot_split(halves(x), yy))
         y = s * (2.0 * y - dot_split(yy, yy))
-    s = scales[-1]
-    x = s * (2.0 * x - dot_split(halves(x), halves(y)))
+    x = scales[-1] * (2.0 * x - dot_split(halves(x), halves(y)))
     for _ in range(polish):
         miss = eye - dot32(a, x)
         x = x + dot_split(halves(x), halves(miss))
     return x
 
-def solve_kernel(low, high, ridge, scale, spots_ref, mine_ref, theirs_ref, out_ref, g_ref):
+
+def unit(n):
+    rows = lax.broadcasted_iota(jnp.int32, (n, n), 0)
+    cols = lax.broadcasted_iota(jnp.int32, (n, n), 1)
+    return jnp.where(rows == cols, 1.0, 0.0).astype(jnp.float32)
+
+
+def slabs(ref, start, rows=256):
+    return jnp.concatenate([ref[start:start + rows], ref[start + rows:start + 2 * rows]], axis=1)
+
+
+def own_kernel(low, high, ridge, mine_ref, x_ref, b_ref):
+    eye = unit(256)
+    x_ref[...] = inverse_of(slabs(mine_ref, 0) + ridge * eye, eye, low, high, 2)
+    b_ref[...] = slabs(mine_ref, 512).T
+
+
+def rest_kernel(low, high, ridge, scale, spots_ref, mine_ref, theirs_ref, x_ref, turned_ref, out_ref, b_ref, r_ref):
+    pick = pl.multiple_of(spots_ref[1], 8)
+
     @pl.when(spots_ref[0] == 0)
     def _():
-        g_ref[0] = mine_ref[...]
-        g_ref[1] = theirs_ref[...]
+        b_ref[...] = slabs(theirs_ref, 512)
+        for k in range(4):
+            r_ref[:, 128 * k:128 * (k + 1)] = mine_ref[pl.ds(512 + 128 * k + pick, 8)]
+
     @pl.when(spots_ref[0] != 0)
     def _():
-        g_ref[0] = theirs_ref[...]
-        g_ref[1] = mine_ref[...]
-    rows = lax.broadcasted_iota(jnp.int32, (256, 256), 0)
-    cols = lax.broadcasted_iota(jnp.int32, (256, 256), 1)
-    eye = jnp.where(rows == cols, 1.0, 0.0).astype(jnp.float32)
-    a = jnp.concatenate([g_ref[0, :256], g_ref[0, 256:512]], axis=1) + ridge * eye
-    b = jnp.concatenate([g_ref[1, :256], g_ref[1, 256:512]], axis=1)
-    c = jnp.concatenate([g_ref[1, 512:768], g_ref[1, 768:]], axis=1) + ridge * eye
-    pick = pl.multiple_of(spots_ref[1], 8)
-    r1 = jnp.concatenate([g_ref[0, pl.ds(512 + pick, 8)], g_ref[0, pl.ds(640 + pick, 8)]], axis=1)
-    r2 = jnp.concatenate([g_ref[0, pl.ds(768 + pick, 8)], g_ref[0, pl.ds(896 + pick, 8)]], axis=1)
-    xa = inverse_of(a, eye, low, high)
-    t = dot32(b, xa)
-    s = c - dot32(t, b, ((1,), (1,)))
-    r2 = r2 - dot32(r1, t, ((1,), (1,)))
-    xs = inverse_of(s, eye, low, high)
-    w2 = dot32(r2, xs)
-    w1 = dot32(r1 - dot32(w2, b), xa)
-    w = scale * jnp.concatenate([w1, w2], axis=1)
+        b_ref[...] = turned_ref[...]
+        for k in range(4):
+            slab = (k + 2) % 4
+            r_ref[:, 128 * k:128 * (k + 1)] = theirs_ref[pl.ds(512 + 128 * slab + pick, 8)]
+
+    eye = unit(256)
+    b = b_ref[...]
+    x = x_ref[...]
+    t = dot32(b, x)
+    s = slabs(theirs_ref, 0) + ridge * eye - dot32(t, b, ((1,), (1,)))
+    right = r_ref[:, 256:] - dot32(r_ref[:, :256], t, ((1,), (1,)))
+    inverse = halves(inverse_of(s, eye, low, high, 0))
+    other = dot_split(halves(right), inverse)
+    for _ in range(2):
+        other = other + dot_split(halves(right - dot32(other, s)), inverse)
+    own = dot32(r_ref[:, :256] - dot32(other, b), x)
+    flip = spots_ref[0] != 0
+    w = scale * jnp.concatenate([jnp.where(flip, other, own), jnp.where(flip, own, other)], axis=1)
     w = jnp.where(spots_ref[2] == 0, w[:4], w[4:])
-    block = spots_ref[3]
     out = w[:, :128]
     for k in range(1, 4):
-        out = jnp.where(block == k, w[:, 128 * k:128 * (k + 1)], out)
+        out = jnp.where(spots_ref[3] == k, w[:, 128 * k:128 * (k + 1)], out)
     out_ref[...] = out
+
 
 def solve(spots, mine, theirs, ridge, scale):
     low = 0.98 * ridge
     high = 1.01 * (256 * 8 + 1) * ridge
+    vmem = pl.BlockSpec(memory_space=pltpu.VMEM)
+    square = jax.ShapeDtypeStruct((256, 256), jnp.float32)
+    params = pltpu.CompilerParams(vmem_limit_bytes=40 * 2**20)
+    x, turned = pl.pallas_call(
+        functools.partial(own_kernel, low, high, ridge),
+        out_shape=[square, square],
+        in_specs=[vmem],
+        out_specs=[vmem, vmem],
+        name="own",
+        cost_estimate=pl.CostEstimate(flops=5 * 10**9, bytes_accessed=10**6, transcendentals=0),
+        compiler_params=params,
+    )(mine)
     return pl.pallas_call(
-        functools.partial(solve_kernel, low, high, ridge, scale),
+        functools.partial(rest_kernel, low, high, ridge, scale),
         out_shape=jax.ShapeDtypeStruct((4, 128), jnp.float32),
-        in_specs=[
-            pl.BlockSpec(memory_space=pltpu.SMEM),
-            pl.BlockSpec(memory_space=pltpu.VMEM),
-            pl.BlockSpec(memory_space=pltpu.VMEM),
-        ],
-        scratch_shapes=[pltpu.VMEM((2, 1024, 128), jnp.float32)],
-        name="solve",
-        compiler_params=pltpu.CompilerParams(vmem_limit_bytes=40 * 2**20),
-    )(spots, mine, theirs)
+        in_specs=[pl.BlockSpec(memory_space=pltpu.SMEM)] + [vmem] * 4,
+        scratch_shapes=[pltpu.VMEM((256, 256), jnp.float32), pltpu.VMEM((8, 512), jnp.float32)],
+        name="rest",
+        compiler_params=params,
+    )(spots, mine, theirs, x, turned)
 
 
 def sine_coefficients(scale):
@@ -138,16 +165,17 @@
     def feature(s, projected):
         f_ref[new, s * part:(s + 1) * part] = cosine_of_turns(projected * turn + phase, scale).astype(jnp.bfloat16)
 
+    def gram_late():
+        late = jnp.concatenate([f_ref[old, :, 256:], y_ref[...]], axis=1)
+        sums = cross(late, f_ref[old])
+        b_ref[...] += sums[:256]
+        r_ref[...] += sums[256:]
+
     def gram_left():
         a_ref[...] += cross(f_ref[old, :, :256], f_ref[old, :, :256])
 
-    def gram_rest(k):
-        cols = slice(k * 256, (k + 1) * 256)
-        b_ref[:, cols] += cross(f_ref[old, :, 256:], f_ref[old, :, cols])
-        r_ref[:, cols] += cross(y_ref[...], f_ref[old, :, cols])
-
     def run(with_features, with_gram):
-        jobs = [gram_left, lambda: gram_rest(0), lambda: gram_rest(1)] if with_gram else []
+        jobs = [gram_late, gram_left] if with_gram else []
         for s in range(rows // part if with_features else 0):
             projected = project(s)
             if jobs:
@@ -179,7 +207,8 @@
 
         def second(ref):
             for k in range(4):
-                ref[256 * k:256 * (k + 1)] = b_ref[:, 128 * k:128 * (k + 1)]
+                slab = (k + 2) % 4
+                ref[256 * k:256 * (k + 1)] = b_ref[:, 128 * slab:128 * (slab + 1)]
 
         @pl.when(spots_ref[0] == 0)
         def _():

time: 76.1 us -> 72.8 us (0.957)
  Pallas kernels: 29.1 us -> 27.3 us
  waiting for transfers between devices: 3.07 us -> 1.54 us
    ppermute x1, waiting for transfers between devices: 1.54 us -> 0.01 us  [sum_over_devices(): return (mine, lax.ppermute(mine, 'core', swap))]
    pallas_call x1, Pallas kernels: 16.8 us -> 15.8 us  [local_gram(): pl.pallas_call(functools.partial(gram_kernel, blocks, part, np.sqrt(2.0 /...]
    pallas_call x1 -> x2, Pallas kernels: 12.3 us -> 11.5 us  [the longest x1 6.9 us: solve(): pl.pallas_call(functools.partial(rest_kernel, low, high, ridge, scale), o...]
  transfers between devices with their start and end apart: 2 -> 2, of which waited for: 2 -> 1; matrix products, arithmetic and copies ran while one was open for 0% -> 0% of each run, Pallas kernels for 0% -> 6%
where the time goes in v2:
time: 72.8 us; the launch traced here: 72.5 us
  blocking collectives  38.7 us (53%)
  Pallas kernels  27.3 us (38%)
  starting transfers between devices  4.79 us (7%)
  waiting for transfers between devices  1.54 us (2%)
    all_to_all x1, blocking collectives, sum_over_devices(): chunks = lax.all_to_all(half.reshape(64, 16, 128), CHIPS, 0, 0, tiled=True)  23.3 us
    pallas_call x1, Pallas kernels, local_gram(): pl.pallas_call(functools.partial(gram_kernel, blocks, part, np.sqrt(2.0 /...  15.8 us
    all_to_all x1, blocking collectives, sum_over_devices(): lax.all_to_all(jnp.broadcast_to(total, (64, 16, 128)), CHIPS, 0, 0, tiled...  15.4 us
    pallas_call x1, Pallas kernels, solve(): pl.pallas_call(functools.partial(rest_kernel, low, high, ridge, scale), o...  6.9 us
    pallas_call x1, Pallas kernels, solve(): pl.pallas_call(functools.partial(own_kernel, low, high, ridge), out_shape...  4.59 us
    ppermute x1, starting transfers between devices, sum_over_devices(): return (mine, lax.ppermute(mine, 'core', swap))  3.3 us
    ppermute x1, waiting for transfers between devices, sum_over_devices(): half = keep + lax.ppermute(send, 'core', swap)  1.54 us
    ppermute x1, starting transfers between devices, sum_over_devices(): half = keep + lax.ppermute(send, 'core', swap)  1.49 us
  transfers between devices with their start and end apart: 2, of which 1 were waited for; matrix products, arithmetic and copies ran while one was open for 0% of the time, Pallas kernels for 6%

profile of v2, /device:TPU:1, one launch (start us, length us, event | category | flops | bytes accessed | tf_op | source)
XLA Modules:
  0.0 72.5 jit_solution(13502915853621210954)
XLA Ops:
  0.0 0.1 pad_add_fusion.spots_ref
  0.1 15.8 %gram.1 = (f32[1024,128]{1,0:T(8,128)S(1)}, f32[1024,128]{1,0:T(8,128)S(1)}) custom-call(s32[4]{0:T(128)S(1)} %pad_add_fusion.spots_ref, bf16[8192,512]{1,0:T(8,128)(2,1)} %x_ref.1, bf16[8192,128]{1,0:T(8,128)(2,1)} %y_ref.1, bf16[512,512]{1,0:T(8,128)(2,1)} %w_ref.1, f32[1,512]{1,0:T(1,128)} %bitcast.12), custom_call_target="tpu_custom_call" | custom-call | tf_op jit(solution)/shard_map/gram/pallas_call | solution.py:231
  15.9 1.5 %collective-permute-start = (f32[1024,128]{1,0:T(8,128)S(1)}, f32[1024,128]{1,0:T(8,128)S(1)}, u32[]{:S(2)}, u32[]{:S(2)}) collective-permute-start(f32[1024,128]{1,0:T(8,128)S(1)} %get-tuple-element.10), channel_id=1, source_target_pairs={{0,4},{4,0},{1,5},{5,1},{2,6},{6,2},{3,7},{7,3},{8,12},{12,8},{9,1... | collective-permute-start | bytes 1572872 | tf_op jit(solution)/shard_map/ppermute | solution.py:256
  17.4 1.5 %collective-permute-done = f32[1024,128]{1,0:T(8,128)S(1)} collective-permute-done((f32[1024,128]{1,0:T(8,128)S(1)}, f32[1024,128]{1,0:T(8,128)S(1)}, u32[]{:S(2)}, u32[]{:S(2)}) %collective-permute-start) | collective-permute-done | bytes 524320 | tf_op jit(solution)/shard_map/ppermute | solution.py:256
  18.9 0.1 add.17
  18.9 23.3 %all_to_all.10 = f32[64,16,128]{2,1,0:T(8,128)S(1)} all-to-all(f32[64,16,128]{2,1,0:T(8,128)S(1)} %bitcast.11), channel_id=1, replica_groups=mesh['z'=4,'x'=4,'core'=2,'y'=4] {'z','x','y'}, dimensions={0} | all-to-all | bytes 1048576 | tf_op jit(solution)/shard_map/all_to_all | solution.py:257
  42.2 0.1 reduce_sum.9
  42.3 15.4 %all_to_all.11 = f32[64,16,128]{2,1,0:T(8,128)S(1)} all-to-all(f32[64,16,128]{2,1,0:T(8,128)S(1)} %broadcast_in_dim.2), channel_id=1, replica_groups=mesh['z'=4,'x'=4,'core'=2,'y'=4] {'z','x','y'}, dimensions={0} | all-to-all | bytes 1048576 | tf_op jit(solution)/shard_map/all_to_all | solution.py:259
  57.7 3.3 %collective-permute-start.1 = (f32[1024,128]{1,0:T(8,128)S(1)}, f32[1024,128]{1,0:T(8,128)S(1)}, u32[]{:S(2)}, u32[]{:S(2)}) collective-permute-start(f32[1024,128]{1,0:T(8,128)S(1)} %bitcast.8), channel_id=1, source_target_pairs={{0,4},{4,0},{1,5},{5,1},{2,6},{6,2},{3,7},{7,3},{8,12},{12,8},{9,1... | collective-permute-start | bytes 1572872 | tf_op jit(solution)/shard_map/ppermute | solution.py:261
  61.0 4.6 %own.1 = (f32[256,256]{1,0:T(8,128)S(1)}, f32[256,256]{1,0:T(8,128)S(1)}) custom-call(f32[1024,128]{1,0:T(8,128)S(1)} %bitcast.9), custom_call_target="tpu_custom_call" | custom-call | flops 5000000000 | bytes 1000000 | tf_op jit(solution)/shard_map/own/pallas_call | solution.py:113
  65.6 0.0 collective-permute-done.1.theirs_ref
  65.6 6.9 %rest.1 = f32[4,128]{1,0:T(4,128)} custom-call(s32[4]{0:T(128)S(1)} %pad_add_fusion.spots_ref, f32[1024,128]{1,0:T(8,128)S(1)} %bitcast.10, f32[1024,128]{1,0:T(8,128)S(1)} %collective-permute-done.1.theirs_ref, f32[256,256]{1,0:T(8,128)S(1)} %get-tuple-element.11.x_ref, f32[256,256]{1,0:T(8,128)S(1)} %get-tuple-element.12.turned_ref), custom_call_target="tpu_custom_call" | custom-call | tf_op jit(solution)/shard_map/rest/pallas_call | solution.py:122
  (1 shorter events, 0.0 us)
Async XLA Ops:
  15.9 3.0 %collective-permute-start = (f32[1024,128]{1,0:T(8,128)S(1)}, f32[1024,128]{1,0:T(8,128)S(1)}, u32[]{:S(2)}, u32[]{:S(2)}) collective-permute-start(f32[1024,128]{1,0:T(8,128)S(1)} %get-tuple-element.10), channel_id=1, source_target_pairs={{0,4},{4,0},{1,5},{5,1},{2,6},{6,2},{3,7},{7,3},{8,12},{12,8},{9,1... | collective-permute-start | bytes 1572872 | tf_op jit(solution)/shard_map/ppermute | solution.py:256
  57.7 7.9 %collective-permute-start.1 = (f32[1024,128]{1,0:T(8,128)S(1)}, f32[1024,128]{1,0:T(8,128)S(1)}, u32[]{:S(2)}, u32[]{:S(2)}) collective-permute-start(f32[1024,128]{1,0:T(8,128)S(1)} %bitcast.8), channel_id=1, source_target_pairs={{0,4},{4,0},{1,5},{5,1},{2,6},{6,2},{3,7},{7,3},{8,12},{12,8},{9,1... | collective-permute-start | bytes 1572872 | tf_op jit(solution)/shard_map/ppermute | solution.py:261

commit v3 on v2

--- a/solution.py
+++ b/solution.py
@@ -151,30 +151,29 @@
     return lax.dot_general(a, b, (((0,), (0,)), ((), ())), preferred_element_type=jnp.float32)
 
 
-def gram_kernel(blocks, part, scale, spots_ref, x_ref, y_ref, w_ref, phase_ref, send_ref, keep_ref, f_ref, a_ref, b_ref, r_ref):
+def gram_kernel(steps, part, scale, spots_ref, x_ref, y_old_ref, y_new_ref, w_ref, phase_ref, send_ref, keep_ref, even_ref, odd_ref, a_ref, b_ref, r_ref):
     step = pl.program_id(0)
-    rows = x_ref.shape[0]
-    new = lax.rem(step, 2)
-    old = 1 - new
+    rows = even_ref.shape[0]
     turn = np.float32(1 / (2 * np.pi))
     phase = phase_ref[...] * turn
 
-    def project(s):
-        return jnp.dot(x_ref[s * part:(s + 1) * part], w_ref[...], preferred_element_type=jnp.float32)
-
-    def feature(s, projected):
-        f_ref[new, s * part:(s + 1) * part] = cosine_of_turns(projected * turn + phase, scale).astype(jnp.bfloat16)
-
-    def gram_late():
-        late = jnp.concatenate([f_ref[old, :, 256:], y_ref[...]], axis=1)
-        sums = cross(late, f_ref[old])
-        b_ref[...] += sums[:256]
-        r_ref[...] += sums[256:]
-
-    def gram_left():
-        a_ref[...] += cross(f_ref[old, :, :256], f_ref[old, :, :256])
-
-    def run(with_features, with_gram):
+    def half_step(start, new_ref, old_ref, y_ref, with_features, with_gram):
+        def project(s):
+            some = x_ref[start + s * part:start + (s + 1) * part]
+            return jnp.dot(some, w_ref[...], preferred_element_type=jnp.float32)
+
+        def feature(s, projected):
+            new_ref[s * part:(s + 1) * part] = cosine_of_turns(projected * turn + phase, scale).astype(jnp.bfloat16)
+
+        def gram_late():
+            late = jnp.concatenate([old_ref[:, 256:], y_ref[...]], axis=1)
+            sums = cross(late, old_ref[...])
+            b_ref[...] += sums[:256]
+            r_ref[...] += sums[256:]
+
+        def gram_left():
+            a_ref[...] += cross(old_ref[:, :256], old_ref[:, :256])
+
         jobs = [gram_late, gram_left] if with_gram else []
         for s in range(rows // part if with_features else 0):
             projected = project(s)
@@ -189,15 +188,17 @@
         a_ref[...] = jnp.zeros_like(a_ref)
         b_ref[...] = jnp.zeros_like(b_ref)
         r_ref[...] = jnp.zeros_like(r_ref)
-        run(True, False)
-
-    @pl.when((step > 0) & (step < blocks))
-    def _():
-        run(True, True)
-
-    @pl.when(step == blocks)
-    def _():
-        run(False, True)
+        half_step(0, even_ref, odd_ref, y_old_ref, True, False)
+        half_step(rows, odd_ref, even_ref, y_new_ref, True, True)
+
+    @pl.when((step > 0) & (step < steps))
+    def _():
+        half_step(0, even_ref, odd_ref, y_old_ref, True, True)
+        half_step(rows, odd_ref, even_ref, y_new_ref, True, True)
+
+    @pl.when(step == steps)
+    def _():
+        half_step(0, even_ref, odd_ref, y_old_ref, False, True)
 
         def first(ref):
             for k in range(2):
@@ -225,30 +226,32 @@
     return pltpu.with_memory_space_constraint(array, pltpu.HBM)
 
 
-def local_gram(spots, inputs, frequencies, phases, targets, rows=1024, part=256):
-    blocks = inputs.shape[0] // rows
+def local_gram(spots, inputs, frequencies, phases, targets, rows=1024, part=512):
+    steps = inputs.shape[0] // (2 * rows)
     count = frequencies.shape[1]
     return pl.pallas_call(
-        functools.partial(gram_kernel, blocks, part, np.sqrt(2.0 / count)),
-        grid=(blocks + 1,),
+        functools.partial(gram_kernel, steps, part, np.sqrt(2.0 / count)),
+        grid=(steps + 1,),
         in_specs=[
             pl.BlockSpec(memory_space=pltpu.SMEM),
-            pl.BlockSpec((rows, 512), lambda i: (jnp.minimum(i, blocks - 1), 0)),
-            pl.BlockSpec((rows, 128), lambda i: (jnp.maximum(i - 1, 0), 0)),
+            pl.BlockSpec((2 * rows, 512), lambda i: (jnp.minimum(i, steps - 1), 0)),
+            pl.BlockSpec((rows, 128), lambda i: (jnp.maximum(2 * i - 1, 0), 0)),
+            pl.BlockSpec((rows, 128), lambda i: (jnp.minimum(2 * i, 2 * steps - 1), 0)),
             pl.BlockSpec((512, 512), lambda i: (0, 0)),
             pl.BlockSpec((1, 512), lambda i: (0, 0)),
         ],
         out_specs=[pl.BlockSpec((1024, 128), lambda i: (0, 0))] * 2,
         out_shape=[jax.ShapeDtypeStruct((1024, 128), jnp.float32)] * 2,
         scratch_shapes=[
-            pltpu.VMEM((2, rows, 512), jnp.bfloat16),
+            pltpu.VMEM((rows, 512), jnp.bfloat16),
+            pltpu.VMEM((rows, 512), jnp.bfloat16),
             pltpu.VMEM((256, 256), jnp.float32),
             pltpu.VMEM((256, 512), jnp.float32),
             pltpu.VMEM((128, 512), jnp.float32),
         ],
         name="gram",
         compiler_params=pltpu.CompilerParams(vmem_limit_bytes=50 * 2**20),
-    )(spots, inputs, *[in_hbm(v) for v in (targets, frequencies, phases.reshape(1, 512))])
+    )(spots, inputs, *[in_hbm(v) for v in (targets, targets, frequencies, phases.reshape(1, 512))])
 
 
 def sum_over_devices(send, keep):

time: 72.8 us -> 72 us (0.989)
  no operation moved by 1% of the time
where the time goes in v3:
time: 72 us; the launch traced here: 71.9 us
  blocking collectives  38.7 us (54%)
  Pallas kernels  26.6 us (37%)
  starting transfers between devices  4.8 us (7%)
  waiting for transfers between devices  1.54 us (2%)
    all_to_all x1, blocking collectives, sum_over_devices(): chunks = lax.all_to_all(half.reshape(64, 16, 128), CHIPS, 0, 0, tiled=True)  23.3 us
    all_to_all x1, blocking collectives, sum_over_devices(): lax.all_to_all(jnp.broadcast_to(total, (64, 16, 128)), CHIPS, 0, 0, tiled...  15.4 us
    pallas_call x1, Pallas kernels, local_gram(): pl.pallas_call(functools.partial(gram_kernel, steps, part, np.sqrt(2.0 /...  15.3 us
    pallas_call x1, Pallas kernels, solve(): pl.pallas_call(functools.partial(rest_kernel, low, high, ridge, scale), o...  6.74 us
    pallas_call x1, Pallas kernels, solve(): pl.pallas_call(functools.partial(own_kernel, low, high, ridge), out_shape...  4.6 us
    ppermute x1, starting transfers between devices, sum_over_devices(): return (mine, lax.ppermute(mine, 'core', swap))  3.3 us
    ppermute x1, waiting for transfers between devices, sum_over_devices(): half = keep + lax.ppermute(send, 'core', swap)  1.54 us
    ppermute x1, starting transfers between devices, sum_over_devices(): half = keep + lax.ppermute(send, 'core', swap)  1.5 us
  transfers between devices with their start and end apart: 2, of which 1 were waited for; matrix products, arithmetic and copies ran while one was open for 0% of the time, Pallas kernels for 6%

profile of v3, /device:TPU:1, one launch (start us, length us, event | category | flops | bytes accessed | tf_op | source)
XLA Modules:
  0.0 71.9 jit_solution(3695226481142011371)
XLA Ops:
  0.0 0.1 pad_add_fusion.spots_ref
  0.1 15.3 %gram.1 = (f32[1024,128]{1,0:T(8,128)S(1)}, f32[1024,128]{1,0:T(8,128)S(1)}) custom-call(s32[4]{0:T(128)S(1)} %pad_add_fusion.spots_ref, bf16[8192,512]{1,0:T(8,128)(2,1)} %x_ref.1, bf16[8192,128]{1,0:T(8,128)(2,1)} %y_new_ref.1, bf16[8192,128]{1,0:T(8,128)(2,1)} %y_new_ref.1, bf16[512,512]{1,0:T(8,128)(2,1)} %w_ref.1, f32[1,512]{1,0:T(1,128)} %bitcast.12), custom_call_target="tpu_custom_call" | custom-call | tf_op jit(solution)/shard_map/gram/pallas_call | solution.py:232
  15.3 1.5 %collective-permute-start = (f32[1024,128]{1,0:T(8,128)S(1)}, f32[1024,128]{1,0:T(8,128)S(1)}, u32[]{:S(2)}, u32[]{:S(2)}) collective-permute-start(f32[1024,128]{1,0:T(8,128)S(1)} %get-tuple-element.10), channel_id=1, source_target_pairs={{0,4},{4,0},{1,5},{5,1},{2,6},{6,2},{3,7},{7,3},{8,12},{12,8},{9,1... | collective-permute-start | bytes 1572872 | tf_op jit(solution)/shard_map/ppermute | solution.py:259
  16.8 1.5 %collective-permute-done = f32[1024,128]{1,0:T(8,128)S(1)} collective-permute-done((f32[1024,128]{1,0:T(8,128)S(1)}, f32[1024,128]{1,0:T(8,128)S(1)}, u32[]{:S(2)}, u32[]{:S(2)}) %collective-permute-start) | collective-permute-done | bytes 524320 | tf_op jit(solution)/shard_map/ppermute | solution.py:259
  18.4 0.1 add.17
  18.4 23.3 %all_to_all.10 = f32[64,16,128]{2,1,0:T(8,128)S(1)} all-to-all(f32[64,16,128]{2,1,0:T(8,128)S(1)} %bitcast.11), channel_id=1, replica_groups=mesh['z'=4,'x'=4,'core'=2,'y'=4] {'z','x','y'}, dimensions={0} | all-to-all | bytes 1048576 | tf_op jit(solution)/shard_map/all_to_all | solution.py:260
  41.7 0.1 reduce_sum.9
  41.8 15.4 %all_to_all.11 = f32[64,16,128]{2,1,0:T(8,128)S(1)} all-to-all(f32[64,16,128]{2,1,0:T(8,128)S(1)} %broadcast_in_dim.2), channel_id=1, replica_groups=mesh['z'=4,'x'=4,'core'=2,'y'=4] {'z','x','y'}, dimensions={0} | all-to-all | bytes 1048576 | tf_op jit(solution)/shard_map/all_to_all | solution.py:262
  57.2 3.3 %collective-permute-start.1 = (f32[1024,128]{1,0:T(8,128)S(1)}, f32[1024,128]{1,0:T(8,128)S(1)}, u32[]{:S(2)}, u32[]{:S(2)}) collective-permute-start(f32[1024,128]{1,0:T(8,128)S(1)} %bitcast.8), channel_id=1, source_target_pairs={{0,4},{4,0},{1,5},{5,1},{2,6},{6,2},{3,7},{7,3},{8,12},{12,8},{9,1... | collective-permute-start | bytes 1572872 | tf_op jit(solution)/shard_map/ppermute | solution.py:264
  60.5 4.6 %own.1 = (f32[256,256]{1,0:T(8,128)S(1)}, f32[256,256]{1,0:T(8,128)S(1)}) custom-call(f32[1024,128]{1,0:T(8,128)S(1)} %bitcast.9), custom_call_target="tpu_custom_call" | custom-call | flops 5000000000 | bytes 1000000 | tf_op jit(solution)/shard_map/own/pallas_call | solution.py:113
  65.1 0.0 collective-permute-done.1.theirs_ref
  65.1 6.7 %rest.1 = f32[4,128]{1,0:T(4,128)} custom-call(s32[4]{0:T(128)S(1)} %pad_add_fusion.spots_ref, f32[1024,128]{1,0:T(8,128)S(1)} %bitcast.10, f32[1024,128]{1,0:T(8,128)S(1)} %collective-permute-done.1.theirs_ref, f32[256,256]{1,0:T(8,128)S(1)} %get-tuple-element.11.x_ref, f32[256,256]{1,0:T(8,128)S(1)} %get-tuple-element.12.turned_ref), custom_call_target="tpu_custom_call" | custom-call | tf_op jit(solution)/shard_map/rest/pallas_call | solution.py:122
  (1 shorter events, 0.0 us)
Async XLA Ops:
  15.3 3.0 %collective-permute-start = (f32[1024,128]{1,0:T(8,128)S(1)}, f32[1024,128]{1,0:T(8,128)S(1)}, u32[]{:S(2)}, u32[]{:S(2)}) collective-permute-start(f32[1024,128]{1,0:T(8,128)S(1)} %get-tuple-element.10), channel_id=1, source_target_pairs={{0,4},{4,0},{1,5},{5,1},{2,6},{6,2},{3,7},{7,3},{8,12},{12,8},{9,1... | collective-permute-start | bytes 1572872 | tf_op jit(solution)/shard_map/ppermute | solution.py:259
  57.2 7.9 %collective-permute-start.1 = (f32[1024,128]{1,0:T(8,128)S(1)}, f32[1024,128]{1,0:T(8,128)S(1)}, u32[]{:S(2)}, u32[]{:S(2)}) collective-permute-start(f32[1024,128]{1,0:T(8,128)S(1)} %bitcast.8), channel_id=1, source_target_pairs={{0,4},{4,0},{1,5},{5,1},{2,6},{6,2},{3,7},{7,3},{8,12},{12,8},{9,1... | collective-permute-start | bytes 1572872 | tf_op jit(solution)/shard_map/ppermute | solution.py:264

commit v4 on v3

--- a/solution.py
+++ b/solution.py
@@ -25,6 +25,10 @@
 def dot_split(a, b):
     (ah, al), (bh, bl) = a, b
     return dot16(ah, bh) + (dot16(ah, bl) + dot16(al, bh))
+
+def dot_rough(a, b):
+    return dot16(a[0], b) + dot16(a[1], b)
+
 
 def spectrum_steps(low, high, small):
     middle = 2.0 / (low + high)
@@ -36,19 +40,23 @@
     return middle, scales
 
 def inverse_of(a, eye, low, high, polish):
-    middle, scales = spectrum_steps(low, high, 1e-3)
+    middle, scales = spectrum_steps(low, high, 1e-2)
     y = middle * a
     yy = halves(y)
     x = (2.0 * middle * scales[0]) * eye - (middle * scales[0]) * y
     y = scales[0] * (2.0 * y - dot_split(yy, yy))
-    for s in scales[1:-1]:
+    for s in scales[1:-3]:
         yy = halves(y)
         x = s * (2.0 * x - dot_split(halves(x), yy))
         y = s * (2.0 * y - dot_split(yy, yy))
-    x = scales[-1] * (2.0 * x - dot_split(halves(x), halves(y)))
+    for s in scales[-3:-1]:
+        yh = y.astype(jnp.bfloat16)
+        x = s * (2.0 * x - dot_rough(halves(x), yh))
+        y = s * (2.0 * y - dot16(yh, yh))
+    x = scales[-1] * (2.0 * x - dot_rough(halves(x), y.astype(jnp.bfloat16)))
     for _ in range(polish):
         miss = eye - dot32(a, x)
-        x = x + dot_split(halves(x), halves(miss))
+        x = x + dot_rough(halves(x), miss.astype(jnp.bfloat16))
     return x
 
 
@@ -64,7 +72,7 @@
 
 def own_kernel(low, high, ridge, mine_ref, x_ref, b_ref):
     eye = unit(256)
-    x_ref[...] = inverse_of(slabs(mine_ref, 0) + ridge * eye, eye, low, high, 2)
+    x_ref[...] = inverse_of(slabs(mine_ref, 0) + ridge * eye, eye, low, high, 1)
     b_ref[...] = slabs(mine_ref, 512).T
 
 
@@ -87,14 +95,19 @@
     eye = unit(256)
     b = b_ref[...]
     x = x_ref[...]
-    t = dot32(b, x)
+    a = slabs(mine_ref, 0) + ridge * eye
+    xx = halves(x)
+    t = dot_split(halves(b), xx)
+    t = t + dot_split(halves(b - dot32(t, a)), xx)
     s = slabs(theirs_ref, 0) + ridge * eye - dot32(t, b, ((1,), (1,)))
     right = r_ref[:, 256:] - dot32(r_ref[:, :256], t, ((1,), (1,)))
     inverse = halves(inverse_of(s, eye, low, high, 0))
     other = dot_split(halves(right), inverse)
     for _ in range(2):
         other = other + dot_split(halves(right - dot32(other, s)), inverse)
-    own = dot32(r_ref[:, :256] - dot32(other, b), x)
+    right = r_ref[:, :256] - dot32(other, b)
+    own = dot_split(halves(right), xx)
+    own = own + dot_split(halves(right - dot32(own, a)), xx)
     flip = spots_ref[0] != 0
     w = scale * jnp.concatenate([jnp.where(flip, other, own), jnp.where(flip, own, other)], axis=1)
     w = jnp.where(spots_ref[2] == 0, w[:4], w[4:])

time: 72 us -> 70.9 us (0.985)
  Pallas kernels: 26.6 us -> 25.4 us
    pallas_call x1, Pallas kernels: 4.6 us -> 2.97 us  [solve(): pl.pallas_call(functools.partial(own_kernel, low, high, ridge), out_shape...]
  transfers between devices with their start and end apart: 2 -> 2, of which waited for: 1 -> 1; matrix products, arithmetic and copies ran while one was open for 0% -> 0% of each run, Pallas kernels for 6% -> 4%
where the time goes in v4:
time: 70.9 us; the launch traced here: 70.7 us
  blocking collectives  38.7 us (55%)
  Pallas kernels  25.4 us (36%)
  starting transfers between devices  4.8 us (7%)
  waiting for transfers between devices  1.54 us (2%)
    all_to_all x1, blocking collectives, sum_over_devices(): chunks = lax.all_to_all(half.reshape(64, 16, 128), CHIPS, 0, 0, tiled=True)  23.3 us
    all_to_all x1, blocking collectives, sum_over_devices(): lax.all_to_all(jnp.broadcast_to(total, (64, 16, 128)), CHIPS, 0, 0, tiled...  15.4 us
    pallas_call x1, Pallas kernels, local_gram(): pl.pallas_call(functools.partial(gram_kernel, steps, part, np.sqrt(2.0 /...  15.3 us
    pallas_call x1, Pallas kernels, solve(): pl.pallas_call(functools.partial(rest_kernel, low, high, ridge, scale), o...  7.18 us
    ppermute x1, starting transfers between devices, sum_over_devices(): return (mine, lax.ppermute(mine, 'core', swap))  3.3 us
    pallas_call x1, Pallas kernels, solve(): pl.pallas_call(functools.partial(own_kernel, low, high, ridge), out_shape...  2.97 us
    ppermute x1, waiting for transfers between devices, sum_over_devices(): half = keep + lax.ppermute(send, 'core', swap)  1.54 us
    ppermute x1, starting transfers between devices, sum_over_devices(): half = keep + lax.ppermute(send, 'core', swap)  1.5 us
  transfers between devices with their start and end apart: 2, of which 1 were waited for; matrix products, arithmetic and copies ran while one was open for 0% of the time, Pallas kernels for 4%

profile of v4, /device:TPU:1, one launch (start us, length us, event | category | flops | bytes accessed | tf_op | source)
XLA Modules:
  0.0 70.7 jit_solution(18292762878678471983)
XLA Ops:
  0.0 0.1 pad_add_fusion.spots_ref
  0.1 15.3 %gram.1 = (f32[1024,128]{1,0:T(8,128)S(1)}, f32[1024,128]{1,0:T(8,128)S(1)}) custom-call(s32[4]{0:T(128)S(1)} %pad_add_fusion.spots_ref, bf16[8192,512]{1,0:T(8,128)(2,1)} %x_ref.1, bf16[8192,128]{1,0:T(8,128)(2,1)} %y_new_ref.1, bf16[8192,128]{1,0:T(8,128)(2,1)} %y_new_ref.1, bf16[512,512]{1,0:T(8,128)(2,1)} %w_ref.1, f32[1,512]{1,0:T(1,128)} %bitcast.12), custom_call_target="tpu_custom_call" | custom-call | tf_op jit(solution)/shard_map/gram/pallas_call | solution.py:245
  15.3 1.5 %collective-permute-start = (f32[1024,128]{1,0:T(8,128)S(1)}, f32[1024,128]{1,0:T(8,128)S(1)}, u32[]{:S(2)}, u32[]{:S(2)}) collective-permute-start(f32[1024,128]{1,0:T(8,128)S(1)} %get-tuple-element.10), channel_id=1, source_target_pairs={{0,4},{4,0},{1,5},{5,1},{2,6},{6,2},{3,7},{7,3},{8,12},{12,8},{9,1... | collective-permute-start | bytes 1572872 | tf_op jit(solution)/shard_map/ppermute | solution.py:272
  16.8 1.5 %collective-permute-done = f32[1024,128]{1,0:T(8,128)S(1)} collective-permute-done((f32[1024,128]{1,0:T(8,128)S(1)}, f32[1024,128]{1,0:T(8,128)S(1)}, u32[]{:S(2)}, u32[]{:S(2)}) %collective-permute-start) | collective-permute-done | bytes 524320 | tf_op jit(solution)/shard_map/ppermute | solution.py:272
  18.4 0.1 add.17
  18.4 23.3 %all_to_all.10 = f32[64,16,128]{2,1,0:T(8,128)S(1)} all-to-all(f32[64,16,128]{2,1,0:T(8,128)S(1)} %bitcast.11), channel_id=1, replica_groups=mesh['z'=4,'x'=4,'core'=2,'y'=4] {'z','x','y'}, dimensions={0} | all-to-all | bytes 1048576 | tf_op jit(solution)/shard_map/all_to_all | solution.py:273
  41.7 0.1 reduce_sum.9
  41.8 15.4 %all_to_all.11 = f32[64,16,128]{2,1,0:T(8,128)S(1)} all-to-all(f32[64,16,128]{2,1,0:T(8,128)S(1)} %broadcast_in_dim.2), channel_id=1, replica_groups=mesh['z'=4,'x'=4,'core'=2,'y'=4] {'z','x','y'}, dimensions={0} | all-to-all | bytes 1048576 | tf_op jit(solution)/shard_map/all_to_all | solution.py:275
  57.2 3.3 %collective-permute-start.1 = (f32[1024,128]{1,0:T(8,128)S(1)}, f32[1024,128]{1,0:T(8,128)S(1)}, u32[]{:S(2)}, u32[]{:S(2)}) collective-permute-start(f32[1024,128]{1,0:T(8,128)S(1)} %bitcast.8), channel_id=1, source_target_pairs={{0,4},{4,0},{1,5},{5,1},{2,6},{6,2},{3,7},{7,3},{8,12},{12,8},{9,1... | collective-permute-start | bytes 1572872 | tf_op jit(solution)/shard_map/ppermute | solution.py:277
  60.5 3.0 %own.1 = (f32[256,256]{1,0:T(8,128)S(1)}, f32[256,256]{1,0:T(8,128)S(1)}) custom-call(f32[1024,128]{1,0:T(8,128)S(1)} %bitcast.9), custom_call_target="tpu_custom_call" | custom-call | flops 5000000000 | bytes 1000000 | tf_op jit(solution)/shard_map/own/pallas_call | solution.py:126
  63.5 0.0 collective-permute-done.1.theirs_ref
  63.5 7.2 %rest.1 = f32[4,128]{1,0:T(4,128)} custom-call(s32[4]{0:T(128)S(1)} %pad_add_fusion.spots_ref, f32[1024,128]{1,0:T(8,128)S(1)} %bitcast.10, f32[1024,128]{1,0:T(8,128)S(1)} %collective-permute-done.1.theirs_ref, f32[256,256]{1,0:T(8,128)S(1)} %get-tuple-element.11.x_ref, f32[256,256]{1,0:T(8,128)S(1)} %get-tuple-element.12.turned_ref), custom_call_target="tpu_custom_call" | custom-call | tf_op jit(solution)/shard_map/rest/pallas_call | solution.py:135
  (1 shorter events, 0.0 us)
Async XLA Ops:
  15.3 3.0 %collective-permute-start = (f32[1024,128]{1,0:T(8,128)S(1)}, f32[1024,128]{1,0:T(8,128)S(1)}, u32[]{:S(2)}, u32[]{:S(2)}) collective-permute-start(f32[1024,128]{1,0:T(8,128)S(1)} %get-tuple-element.10), channel_id=1, source_target_pairs={{0,4},{4,0},{1,5},{5,1},{2,6},{6,2},{3,7},{7,3},{8,12},{12,8},{9,1... | collective-permute-start | bytes 1572872 | tf_op jit(solution)/shard_map/ppermute | solution.py:272
  57.2 6.3 %collective-permute-start.1 = (f32[1024,128]{1,0:T(8,128)S(1)}, f32[1024,128]{1,0:T(8,128)S(1)}, u32[]{:S(2)}, u32[]{:S(2)}) collective-permute-start(f32[1024,128]{1,0:T(8,128)S(1)} %bitcast.8), channel_id=1, source_target_pairs={{0,4},{4,0},{1,5},{5,1},{2,6},{6,2},{3,7},{7,3},{8,12},{12,8},{9,1... | collective-permute-start | bytes 1572872 | tf_op jit(solution)/shard_map/ppermute | solution.py:277

commit v5 on v4

--- a/solution.py
+++ b/solution.py
@@ -103,8 +103,8 @@
     right = r_ref[:, 256:] - dot32(r_ref[:, :256], t, ((1,), (1,)))
     inverse = halves(inverse_of(s, eye, low, high, 0))
     other = dot_split(halves(right), inverse)
-    for _ in range(2):
-        other = other + dot_split(halves(right - dot32(other, s)), inverse)
+    other = other + dot_split(halves(right - dot_split(halves(other), halves(s))), inverse)
+    other = other + dot_split(halves(right - dot32(other, s)), inverse)
     right = r_ref[:, :256] - dot32(other, b)
     own = dot_split(halves(right), xx)
     own = own + dot_split(halves(right - dot32(own, a)), xx)
@@ -164,35 +164,36 @@
     return lax.dot_general(a, b, (((0,), (0,)), ((), ())), preferred_element_type=jnp.float32)
 
 
-def gram_kernel(steps, part, scale, spots_ref, x_ref, y_old_ref, y_new_ref, w_ref, phase_ref, send_ref, keep_ref, even_ref, odd_ref, a_ref, b_ref, r_ref):
+def gram_kernel(steps, part, scale, spots_ref, x_ref, y_old_ref, y_new_ref, y_last_ref, w_ref, phase_ref, send_ref, keep_ref, even_ref, odd_ref, a_ref, b_ref, r_ref):
     step = pl.program_id(0)
     rows = even_ref.shape[0]
     turn = np.float32(1 / (2 * np.pi))
     phase = phase_ref[...] * turn
 
-    def half_step(start, new_ref, old_ref, y_ref, with_features, with_gram):
-        def project(s):
-            some = x_ref[start + s * part:start + (s + 1) * part]
-            return jnp.dot(some, w_ref[...], preferred_element_type=jnp.float32)
-
-        def feature(s, projected):
-            new_ref[s * part:(s + 1) * part] = cosine_of_turns(projected * turn + phase, scale).astype(jnp.bfloat16)
-
-        def gram_late():
-            late = jnp.concatenate([old_ref[:, 256:], y_ref[...]], axis=1)
-            sums = cross(late, old_ref[...])
-            b_ref[...] += sums[:256]
-            r_ref[...] += sums[256:]
-
-        def gram_left():
-            a_ref[...] += cross(old_ref[:, :256], old_ref[:, :256])
-
-        jobs = [gram_late, gram_left] if with_gram else []
-        for s in range(rows // part if with_features else 0):
-            projected = project(s)
-            if jobs:
-                jobs.pop(0)()
-            feature(s, projected)
+    def advance(features, gram):
+        jobs = []
+        if gram:
+            old_ref, y_ref, first_row, count = gram
+            some = slice(first_row, first_row + count)
+
+            def gram_late():
+                late = jnp.concatenate([old_ref[some, 256:], y_ref[some]], axis=1)
+                sums = cross(late, old_ref[some])
+                b_ref[...] += sums[:256]
+                r_ref[...] += sums[256:]
+
+            def gram_left():
+                a_ref[...] += cross(old_ref[some, :256], old_ref[some, :256])
+
+            jobs = [gram_late, gram_left]
+        if features:
+            start, new_ref, into, count = features
+            for s in range(0, count, part):
+                projected = jnp.dot(x_ref[start + s:start + s + part], w_ref[...], preferred_element_type=jnp.float32)
+                if jobs:
+                    jobs.pop(0)()
+                made = cosine_of_turns(projected * turn + phase, scale).astype(jnp.bfloat16)
+                new_ref[into + s:into + s + part] = made
         for job in jobs:
             job()
 
@@ -201,17 +202,21 @@
         a_ref[...] = jnp.zeros_like(a_ref)
         b_ref[...] = jnp.zeros_like(b_ref)
         r_ref[...] = jnp.zeros_like(r_ref)
-        half_step(0, even_ref, odd_ref, y_old_ref, True, False)
-        half_step(rows, odd_ref, even_ref, y_new_ref, True, True)
-
-    @pl.when((step > 0) & (step < steps))
-    def _():
-        half_step(0, even_ref, odd_ref, y_old_ref, True, True)
-        half_step(rows, odd_ref, even_ref, y_new_ref, True, True)
-
-    @pl.when(step == steps)
-    def _():
-        half_step(0, even_ref, odd_ref, y_old_ref, False, True)
+        advance((0, even_ref, 0, part), None)
+        advance((part, even_ref, part, rows - part), (even_ref, y_new_ref, 0, part))
+        advance((rows, odd_ref, 0, rows), (even_ref, y_new_ref, part, rows - part))
+
+    @pl.when((step > 0) & (step < steps - 1))
+    def _():
+        advance((0, even_ref, 0, rows), (odd_ref, y_old_ref, 0, rows))
+        advance((rows, odd_ref, 0, rows), (even_ref, y_new_ref, 0, rows))
+
+    @pl.when(step == steps - 1)
+    def _():
+        advance((0, even_ref, 0, rows), (odd_ref, y_old_ref, 0, rows))
+        advance((rows, odd_ref, 0, rows - part), (even_ref, y_new_ref, 0, rows))
+        advance((2 * rows - part, odd_ref, rows - part, part), (odd_ref, y_last_ref, 0, rows - part))
+        advance(None, (odd_ref, y_last_ref, rows - part, part))
 
         def first(ref):
             for k in range(2):
@@ -244,12 +249,13 @@
     count = frequencies.shape[1]
     return pl.pallas_call(
         functools.partial(gram_kernel, steps, part, np.sqrt(2.0 / count)),
-        grid=(steps + 1,),
+        grid=(steps,),
         in_specs=[
             pl.BlockSpec(memory_space=pltpu.SMEM),
-            pl.BlockSpec((2 * rows, 512), lambda i: (jnp.minimum(i, steps - 1), 0)),
+            pl.BlockSpec((2 * rows, 512), lambda i: (i, 0)),
             pl.BlockSpec((rows, 128), lambda i: (jnp.maximum(2 * i - 1, 0), 0)),
-            pl.BlockSpec((rows, 128), lambda i: (jnp.minimum(2 * i, 2 * steps - 1), 0)),
+            pl.BlockSpec((rows, 128), lambda i: (2 * i, 0)),
+            pl.BlockSpec((rows, 128), lambda i: (2 * steps - 1, 0)),
             pl.BlockSpec((512, 512), lambda i: (0, 0)),
             pl.BlockSpec((1, 512), lambda i: (0, 0)),
         ],
@@ -264,7 +270,7 @@
         ],
         name="gram",
         compiler_params=pltpu.CompilerParams(vmem_limit_bytes=50 * 2**20),
-    )(spots, inputs, *[in_hbm(v) for v in (targets, targets, frequencies, phases.reshape(1, 512))])
+    )(spots, inputs, *[in_hbm(v) for v in (targets, targets, targets, frequencies, phases.reshape(1, 512))])
 
 
 def sum_over_devices(send, keep):

time: 70.9 us -> 70.3 us (level)
  no operation moved by 1% of the time
where the time goes in v5:
time: 70.3 us; the launch traced here: 70.1 us
  blocking collectives  38.7 us (55%)
  Pallas kernels  24.9 us (35%)
  starting transfers between devices  4.78 us (7%)
  waiting for transfers between devices  1.54 us (2%)
    all_to_all x1, blocking collectives, sum_over_devices(): chunks = lax.all_to_all(half.reshape(64, 16, 128), CHIPS, 0, 0, tiled=True)  23.3 us
    all_to_all x1, blocking collectives, sum_over_devices(): lax.all_to_all(jnp.broadcast_to(total, (64, 16, 128)), CHIPS, 0, 0, tiled...  15.4 us
    pallas_call x1, Pallas kernels, local_gram(): pl.pallas_call(functools.partial(gram_kernel, steps, part, np.sqrt(2.0 /...  15 us
    pallas_call x1, Pallas kernels, solve(): pl.pallas_call(functools.partial(rest_kernel, low, high, ridge, scale), o...  6.86 us
    ppermute x1, starting transfers between devices, sum_over_devices(): return (mine, lax.ppermute(mine, 'core', swap))  3.3 us
    pallas_call x1, Pallas kernels, solve(): pl.pallas_call(functools.partial(own_kernel, low, high, ridge), out_shape...  2.97 us
    ppermute x1, waiting for transfers between devices, sum_over_devices(): half = keep + lax.ppermute(send, 'core', swap)  1.54 us
    ppermute x1, starting transfers between devices, sum_over_devices(): half = keep + lax.ppermute(send, 'core', swap)  1.48 us
  transfers between devices with their start and end apart: 2, of which 1 were waited for; matrix products, arithmetic and copies ran while one was open for 0% of the time, Pallas kernels for 4%

profile of v5, /device:TPU:1, one launch (start us, length us, event | category | flops | bytes accessed | tf_op | source)
XLA Modules:
  0.0 70.1 jit_solution(12385695804553789622)
XLA Ops:
  0.0 0.1 pad_add_fusion.spots_ref
  0.1 15.0 %gram.1 = (f32[1024,128]{1,0:T(8,128)S(1)}, f32[1024,128]{1,0:T(8,128)S(1)}) custom-call(s32[4]{0:T(128)S(1)} %pad_add_fusion.spots_ref, bf16[8192,512]{1,0:T(8,128)(2,1)} %x_ref.1, bf16[8192,128]{1,0:T(8,128)(2,1)} %y_last_ref.1, bf16[8192,128]{1,0:T(8,128)(2,1)} %y_last_ref.1, bf16[8192,128]{1,0:T(8,128)(2,1)} %y_last_ref.1, bf16[512,512]{1,0:T(8,128)(2,1)} %w_ref.1, ...), custom_call_target="tpu_custom_call" | custom-call | tf_op jit(solution)/shard_map/gram/pallas_call | solution.py:250
  15.1 1.5 %collective-permute-start = (f32[1024,128]{1,0:T(8,128)S(1)}, f32[1024,128]{1,0:T(8,128)S(1)}, u32[]{:S(2)}, u32[]{:S(2)}) collective-permute-start(f32[1024,128]{1,0:T(8,128)S(1)} %get-tuple-element.10), channel_id=1, source_target_pairs={{0,4},{4,0},{1,5},{5,1},{2,6},{6,2},{3,7},{7,3},{8,12},{12,8},{9,1... | collective-permute-start | bytes 1572872 | tf_op jit(solution)/shard_map/ppermute | solution.py:278
  16.6 1.5 %collective-permute-done = f32[1024,128]{1,0:T(8,128)S(1)} collective-permute-done((f32[1024,128]{1,0:T(8,128)S(1)}, f32[1024,128]{1,0:T(8,128)S(1)}, u32[]{:S(2)}, u32[]{:S(2)}) %collective-permute-start) | collective-permute-done | bytes 524320 | tf_op jit(solution)/shard_map/ppermute | solution.py:278
  18.1 0.1 add.17
  18.2 23.3 %all_to_all.10 = f32[64,16,128]{2,1,0:T(8,128)S(1)} all-to-all(f32[64,16,128]{2,1,0:T(8,128)S(1)} %bitcast.11), channel_id=1, replica_groups=mesh['z'=4,'x'=4,'core'=2,'y'=4] {'z','x','y'}, dimensions={0} | all-to-all | bytes 1048576 | tf_op jit(solution)/shard_map/all_to_all | solution.py:279
  41.5 0.1 reduce_sum.9
  41.6 15.4 %all_to_all.11 = f32[64,16,128]{2,1,0:T(8,128)S(1)} all-to-all(f32[64,16,128]{2,1,0:T(8,128)S(1)} %broadcast_in_dim.2), channel_id=1, replica_groups=mesh['z'=4,'x'=4,'core'=2,'y'=4] {'z','x','y'}, dimensions={0} | all-to-all | bytes 1048576 | tf_op jit(solution)/shard_map/all_to_all | solution.py:281
  57.0 3.3 %collective-permute-start.1 = (f32[1024,128]{1,0:T(8,128)S(1)}, f32[1024,128]{1,0:T(8,128)S(1)}, u32[]{:S(2)}, u32[]{:S(2)}) collective-permute-start(f32[1024,128]{1,0:T(8,128)S(1)} %bitcast.8), channel_id=1, source_target_pairs={{0,4},{4,0},{1,5},{5,1},{2,6},{6,2},{3,7},{7,3},{8,12},{12,8},{9,1... | collective-permute-start | bytes 1572872 | tf_op jit(solution)/shard_map/ppermute | solution.py:283
  60.3 3.0 %own.1 = (f32[256,256]{1,0:T(8,128)S(1)}, f32[256,256]{1,0:T(8,128)S(1)}) custom-call(f32[1024,128]{1,0:T(8,128)S(1)} %bitcast.9), custom_call_target="tpu_custom_call" | custom-call | flops 5000000000 | bytes 1000000 | tf_op jit(solution)/shard_map/own/pallas_call | solution.py:126
  63.3 0.0 collective-permute-done.1.theirs_ref
  63.3 6.9 %rest.1 = f32[4,128]{1,0:T(4,128)} custom-call(s32[4]{0:T(128)S(1)} %pad_add_fusion.spots_ref, f32[1024,128]{1,0:T(8,128)S(1)} %bitcast.10, f32[1024,128]{1,0:T(8,128)S(1)} %collective-permute-done.1.theirs_ref, f32[256,256]{1,0:T(8,128)S(1)} %get-tuple-element.11.x_ref, f32[256,256]{1,0:T(8,128)S(1)} %get-tuple-element.12.turned_ref), custom_call_target="tpu_custom_call" | custom-call | tf_op jit(solution)/shard_map/rest/pallas_call | solution.py:135
  (1 shorter events, 0.0 us)
Async XLA Ops:
  15.1 3.0 %collective-permute-start = (f32[1024,128]{1,0:T(8,128)S(1)}, f32[1024,128]{1,0:T(8,128)S(1)}, u32[]{:S(2)}, u32[]{:S(2)}) collective-permute-start(f32[1024,128]{1,0:T(8,128)S(1)} %get-tuple-element.10), channel_id=1, source_target_pairs={{0,4},{4,0},{1,5},{5,1},{2,6},{6,2},{3,7},{7,3},{8,12},{12,8},{9,1... | collective-permute-start | bytes 1572872 | tf_op jit(solution)/shard_map/ppermute | solution.py:278
  57.0 6.3 %collective-permute-start.1 = (f32[1024,128]{1,0:T(8,128)S(1)}, f32[1024,128]{1,0:T(8,128)S(1)}, u32[]{:S(2)}, u32[]{:S(2)}) collective-permute-start(f32[1024,128]{1,0:T(8,128)S(1)} %bitcast.8), channel_id=1, source_target_pairs={{0,4},{4,0},{1,5},{5,1},{2,6},{6,2},{3,7},{7,3},{8,12},{12,8},{9,1... | collective-permute-start | bytes 1572872 | tf_op jit(solution)/shard_map/ppermute | solution.py:283
